TPU v7x, 32 devices: a whole 2x2x4 slice. The times are simulated.
32 devices in a mesh: query: 2 (over x), corpus: 16 (over z, y, core).
Axes of the slice: x: 2, y: 2, z: 4, core: 2. Of those that a mesh axis runs over, the one named last changes fastest.
Arguments:
- clean_feats: bfloat16 [2, 2, 512, 320], P('query', None, 'corpus'), may hold values from -6 to 6
- noise_draw: bfloat16 [2, 2, 512, 320], P('query', None, 'corpus'), may hold values from -6 to 6
- timesteps: int32 [2, 2], P('query'), may hold values from 0 to 999
- weight_in: bfloat16 [2, 320, 320], P(None, None, 'corpus'), may hold values from -0.3125 to 0.3125
- weight_ffin: bfloat16 [2, 320, 2560], P(None, None, 'corpus'), may hold values from -0.3125 to 0.3125
- weight_ffout: bfloat16 [2, 1280, 320], P(None, None, 'corpus'), may hold values from -0.15625 to 0.15625
- weight_out: bfloat16 [2, 320, 320], P(None, None, 'corpus'), may hold values from -0.3125 to 0.3125
- norm_gain: float32 [2, 320], replicated, may hold values from 0.5 to 1.5
- norm_bias: float32 [2, 320], replicated, may hold values from -3 to 3
- sketch_cin: bfloat16 [2, 3, 320, 16], replicated, may hold values from -0.3125 to 0.3125
- sketch_fin: bfloat16 [2, 1280, 16], replicated, may hold values from -0.15625 to 0.15625
- sketch_cout: bfloat16 [2, 3, 320, 16], replicated, may hold values from -0.3125 to 0.3125
- sketch_fout: bfloat16 [2, 2560, 16], replicated, may hold values from -0.125 to 0.125
- precond: float32 [8, 256, 256], P('query'), as said below
- store_grads: bfloat16 [8192, 2048], P(('query', 'corpus')), may hold values from -6 to 6
- store_scale: float32 [8192], P(('query', 'corpus')), may hold values from 0.002 to 0.03
Outputs:
- scores: float32 [2, 8192], P(None, ('query', 'corpus'))
Inputs may be any that keep to these rules, and one draw needn't show every extreme that they name: `precond`: each layer's matrix is symmetric with a diagonal between 1 and 2.
All inputs are finite; a program needn't handle non-finite values.
Results may differ from a plain program's by a relative error of at most 0.0085.
Values may be sent and summed in bfloat16 or wider, within the bound.
A program may use at most 64 MiB of HBM per device.

v0:
```python
import math
import jax
import jax.numpy as jnp
from jax import lax
from jax.sharding import PartitionSpec as P

plan_len = 1000


def noise_levels(timesteps):
    steps = jnp.arange(plan_len, dtype=jnp.float32)
    rooted = math.sqrt(0.00085) + (math.sqrt(0.012) - math.sqrt(0.00085)) * steps / (plan_len - 1)
    terms = jnp.log1p(-rooted * rooted)
    reached = jnp.arange(plan_len, dtype=jnp.int32) <= timesteps[..., None]
    picked = jnp.exp(jnp.sum(jnp.where(reached, terms, jnp.zeros_like(terms)), axis=-1))
    return (jnp.sqrt(picked), jnp.sqrt(1.0 - picked))


def gelu_parts(gate):
    cumul = 0.5 * (1.0 + jax.scipy.special.erf(gate / math.sqrt(2.0)))
    density = jnp.exp(-0.5 * gate * gate) / math.sqrt(2.0 * math.pi)
    return (gate * cumul, cumul + gate * density)


def contract_back(delta, weight):
    return lax.dot_general(
        delta, weight, (((1,), (1,)), ((), ())), preferred_element_type=jnp.float32
    )


def block_forward(residual_stream, weights, scale_gain, shift_bias):
    weight_in, weight_ffin, weight_ffout, weight_out = weights
    hidden = weight_ffout.shape[0]
    residual_reduced = residual_stream.astype(jnp.bfloat16)
    inner = jnp.dot(residual_reduced, weight_in, preferred_element_type=jnp.float32)
    centred_input = inner - jnp.mean(inner, axis=-1, keepdims=True)
    inverse_deviation = lax.rsqrt(
        jnp.mean(centred_input * centred_input, axis=-1, keepdims=True) + 1e-05
    )
    standardized_input = centred_input * inverse_deviation
    normalized_input = (standardized_input * scale_gain + shift_bias).astype(jnp.bfloat16)
    projected = jnp.dot(normalized_input, weight_ffin, preferred_element_type=jnp.float32)
    value_output = projected[:, :hidden]
    gate = projected[:, hidden:]
    gelu_result, gelu_derivative = gelu_parts(gate)
    mixed_hidden = (value_output * gelu_result).astype(jnp.bfloat16)
    inner_two = inner + jnp.dot(mixed_hidden, weight_ffout, preferred_element_type=jnp.float32)
    inner_reduced = inner_two.astype(jnp.bfloat16)
    residual_stream = residual_stream + jnp.dot(
        inner_reduced, weight_out, preferred_element_type=jnp.float32
    )
    return (
        residual_stream,
        (
            residual_reduced,
            standardized_input,
            inverse_deviation,
            normalized_input,
            value_output,
            gelu_result,
            gelu_derivative,
            mixed_hidden,
            inner_reduced,
        ),
    )


def block_backward(dstream, saved_activations, weights, scale_gain):
    weight_in, weight_ffin, weight_ffout, weight_out = weights
    (
        residual_reduced,
        standardized_input,
        inverse_deviation,
        normalized_input,
        value_output,
        gelu_result,
        gelu_derivative,
        mixed_hidden,
        inner_reduced,
    ) = saved_activations
    dout_low = dstream.astype(jnp.bfloat16)
    second_inner_gradient = contract_back(dout_low, weight_out)
    dtwo_low = second_inner_gradient.astype(jnp.bfloat16)
    dmixed = contract_back(dtwo_low, weight_ffout)
    dproj_low = jnp.concatenate(
        [dmixed * gelu_result, dmixed * value_output * gelu_derivative], axis=-1
    ).astype(jnp.bfloat16)
    dnormed = contract_back(dproj_low, weight_ffin)
    scaled_hidden = dnormed * scale_gain
    inner_gradient = second_inner_gradient + inverse_deviation * (
        scaled_hidden
        - jnp.mean(scaled_hidden, axis=-1, keepdims=True)
        - standardized_input * jnp.mean(scaled_hidden * standardized_input, axis=-1, keepdims=True)
    )
    dinner_low = inner_gradient.astype(jnp.bfloat16)
    dstream = dstream + contract_back(dinner_low, weight_in)
    records = [
        (residual_reduced, dinner_low),
        (normalized_input, dproj_low),
        (mixed_hidden, dtwo_low),
        (inner_reduced, dout_low),
    ]
    return (dstream, records)


def project_layer(inputs, deltas, sketch_in, sketch_out, samples):
    left = jnp.dot(inputs, sketch_in, preferred_element_type=jnp.float32)
    right = jnp.dot(deltas, sketch_out, preferred_element_type=jnp.float32)
    left = left.reshape(samples, -1, left.shape[-1])
    right = right.reshape(samples, -1, right.shape[-1])
    outer = jnp.einsum("srk,srj->skj", left, right, precision=lax.Precision.HIGHEST)
    return outer.reshape(samples, -1)


def sketches_of(block, sketch_cin, sketch_fin, sketch_cout, sketch_fout):
    return [
        (sketch_cin[block, 0], sketch_cout[block, 0]),
        (sketch_cin[block, 1], sketch_fout[block]),
        (sketch_fin[block], sketch_cout[block, 1]),
        (sketch_cin[block, 2], sketch_cout[block, 2]),
    ]


def on_device(
    clean_feats,
    noise_draw,
    timesteps,
    weight_in,
    weight_ffin,
    weight_ffout,
    weight_out,
    norm_gain,
    norm_bias,
    sketch_cin,
    sketch_fin,
    sketch_cout,
    sketch_fout,
    precond,
    store_grads,
    store_scale,
):
    samples = clean_feats.shape[0]
    positions = clean_feats.shape[2] * lax.axis_size("corpus")
    loss_scale = 1.0 / math.sqrt(clean_feats.shape[1] * positions)
    blocks = weight_in.shape[0]
    signal, spread = noise_levels(timesteps)
    noise_rows = noise_draw.astype(jnp.float32)
    residual_stream = (
        signal[:, :, None, None] * clean_feats.astype(jnp.float32)
        + spread[:, :, None, None] * noise_rows
    )
    residual_stream = residual_stream.reshape(-1, residual_stream.shape[-1])
    noise_rows = noise_rows.reshape(-1, noise_rows.shape[-1])
    gathered = (
        lax.all_gather(weight_in, "corpus", axis=2, tiled=True),
        lax.all_gather(weight_ffin, "corpus", axis=2, tiled=True),
        lax.all_gather(weight_ffout, "corpus", axis=2, tiled=True),
        lax.all_gather(weight_out, "corpus", axis=2, tiled=True),
    )

    def fetch_forward(block):
        return tuple((member[block] for member in gathered))

    def fetch_backward(block):
        return tuple((member[block] for member in gathered))

    saved_all = []
    for block in range(blocks):
        residual_stream, saved_activations = block_forward(
            residual_stream, fetch_forward(block), norm_gain[block], norm_bias[block]
        )
        saved_all.append(saved_activations)
    dstream = (residual_stream - noise_rows) * loss_scale
    layers = [None] * (4 * blocks)
    for block in reversed(range(blocks)):
        dstream, records = block_backward(
            dstream, saved_all[block], fetch_backward(block), norm_gain[block]
        )
        pairs = sketches_of(block, sketch_cin, sketch_fin, sketch_cout, sketch_fout)
        for index in range(4):
            layers[4 * block + index] = project_layer(
                records[index][0], records[index][1], pairs[index][0], pairs[index][1], samples
            )
    partial_grads = jnp.stack(layers, axis=1)
    totals = lax.psum(partial_grads, "corpus")
    routed = lax.all_to_all(totals, "query", split_axis=1, concat_axis=0, tiled=True)
    owned = jnp.einsum("qlk,lkj->qlj", routed, precond, precision=lax.Precision.HIGHEST).astype(
        jnp.bfloat16
    )
    preconditioned = lax.all_gather(owned, "query", axis=1, tiled=True)
    flat = preconditioned.reshape(preconditioned.shape[0], -1)
    raw = lax.dot_general(
        flat, store_grads, (((1,), (1,)), ((), ())), preferred_element_type=jnp.float32
    )
    return raw * store_scale[None, :]


def solution(mesh):
    placed = (
        P("query", None, "corpus", None),
        P("query", None, "corpus", None),
        P("query", None),
        P(None, None, "corpus"),
        P(None, None, "corpus"),
        P(None, None, "corpus"),
        P(None, None, "corpus"),
        P(),
        P(),
        P(),
        P(),
        P(),
        P(),
        P("query", None, None),
        P(("query", "corpus"), None),
        P(("query", "corpus")),
    )
    return jax.shard_map(
        on_device,
        mesh=mesh,
        in_specs=placed,
        out_specs=P(None, ("query", "corpus")),
        check_vma=False,
    )
```

profile of v0, /device:TPU:0, one launch (start us, length us, event | category | flops | bytes accessed | tf_op | source)
XLA Modules:
  0.0 167.8 jit_solution(465755251760985908)
XLA Ops:
  6.5 0.7 all-gather.5.cloned.1.call-update
  7.3 0.7 all-gather.3.cloned.1.call-update
  8.0 25.0 %all_gather.15 = bf16[2,320,320]{1,0,2:T(2,128)(2,1)S(1)} all-gather(bf16[2,320,20]{1,0,2:T(2,128)(2,1)} %param.19), channel_id=1, replica_groups=mesh['query'=2,'corpus'=16] {'corpus'}, dimensions={2}, use_global_device_ids=true | all-gather | bytes 435200 | tf_op jit(solution)/shard_map/all_gather | solution.py:155
  33.0 0.7 fusion.105
  33.7 0.9 copy.52
  34.6 19.7 %all_gather.18 = bf16[2,320,320]{1,0,2:T(2,128)(2,1)S(1)} all-gather(bf16[2,320,20]{1,0,2:T(2,128)(2,1)S(1)} %copy-done.12), channel_id=1, replica_groups=mesh['query'=2,'corpus'=16] {'corpus'}, dimensions={2}, use_global_device_ids=true | all-gather | bytes 435200 | tf_op jit(solution)/shard_map/all_gather | solution.py:158
  54.3 0.7 fusion.104
  55.0 0.9 copy.54
  55.9 0.9 copy.55
  56.8 0.9 copy.57
  57.7 0.6 slice_reduce_fusion
  58.6 0.7 fusion.102
  59.8 0.8 fusion.79
  60.7 0.6 copy-done.4
  61.3 0.8 fusion.76
  62.2 5.7 %fusion.103 = (bf16[1,1280,320]{1,0,2:T(2,128)(2,1)}, bf16[1,1280,320]{1,0,2:T(2,128)(2,1)S(1)}) fusion(bf16[2,1280,320]{1,0,2:T(2,128)(2,1)} %all-gather.5.cloned.1.call-done), kind=kLoop, calls=%fused_computation.161 | loop fusion | bytes 3276800 | tf_op jit(solution)/shard_map/slice | solution.py:162
  67.9 36.5 %all-gather.3.cloned.1.call-done = bf16[2,320,2560]{1,2,0:T(8,128)(2,1)} async-done(((bf16[2,320,160]{1,2,0:T(8,128)(2,1)}), bf16[2,320,2560]{1,2,0:T(8,128)(2,1)}) %all-gather.3.cloned.1.call-update) | async-done | bytes 3276816 | tf_op jit(solution)/shard_map/all_gather | solution.py:156
  104.3 2.5 %fusion.1 = f32[64,2560]{1,0:T(8,128)S(1)} fusion(bf16[64,320]{1,0:T(8,128)(2,1)} %copy-done.4, bf16[2,320,2560]{1,2,0:T(8,128)(2,1)} %all-gather.3.cloned.1.call-done), kind=kOutput, calls=%fused_computation.3 | convolution fusion | flops 104857600 | bytes 2670592 | tf_op jit(solution)/shard_map/dot_general | solution.py:42
  108.2 0.7 fusion.3
  116.3 32.2 %psum.7 = f32[1,8,256]{2,0,1:T(1,128)S(1)} all-reduce(f32[1,8,256]{2,0,1:T(1,128)S(1)} %constant_dynamic-update-slice_fusion), channel_id=1, replica_groups=mesh['query'=2,'corpus'=16] {'corpus'}, use_global_device_ids=true, to_apply=%region_9.10 | all-reduce | flops 2048 | bytes 16384 | tf_op jit(solution)/shard_map/psum | solution.py:185
  148.6 6.3 %all_to_all.12 = f32[1,8,256]{2,0,1:T(1,128)S(1)} all-to-all(f32[1,8,256]{2,0,1:T(1,128)S(1)} %psum.7), channel_id=1, replica_groups=mesh['query'=2,'corpus'=16] {'query'}, dimensions={1} | all-to-all | bytes 16384 | tf_op jit(solution)/shard_map/all_to_all | solution.py:186
  155.0 0.6 fusion.11
  155.6 4.3 %all_gather.19 = bf16[2,8,256]{2,0,1:T(2,128)(2,1)S(1)} all-gather(bf16[2,4,256]{2,0,1:T(2,128)(2,1)S(1)} %fusion.11), channel_id=1, replica_groups=mesh['query'=2,'corpus'=16] {'query'}, dimensions={1}, use_global_device_ids=true | all-gather | bytes 12288 | tf_op jit(solution)/shard_map/all_gather | solution.py:190
  160.0 1.0 convolution_multiply_fusion
  (119 shorter events, 9.5 us)
Async XLA Ops:
  6.5 148.5 %copy-start = (f32[4,256,256]{2,1,0:T(8,128)S(1)}, f32[4,256,256]{2,1,0:T(8,128)}, u32[]{:S(2)}) copy-start(f32[4,256,256]{2,1,0:T(8,128)} %param.29) | copy-start | bytes 3145732
  6.5 28.1 %copy-start.12 = (bf16[2,320,20]{1,0,2:T(2,128)(2,1)S(1)}, bf16[2,320,20]{1,0,2:T(2,128)(2,1)}, u32[]{:S(2)}) copy-start(bf16[2,320,20]{1,0,2:T(2,128)(2,1)} %param.22) | copy-start | bytes 76804
  6.5 55.6 %all-gather.5.cloned.1.call-start = ((), (), s32[]{:S(2)}) async-start(), calls=%async_computation.2 | async-start | bytes 1740800 | tf_op jit(solution)/shard_map/all_gather | solution.py:157
  7.3 97.1 %all-gather.3.cloned.1.call-start = ((), (), s32[]{:S(2)}) async-start(), calls=%async_computation.1 | async-start | bytes 4177920 | tf_op jit(solution)/shard_map/all_gather | solution.py:156
  54.3 3.4 %copy-start.16 = (f32[2,320]{1,0:T(2,128)S(1)}, f32[2,320]{1,0:T(2,128)}, u32[]{:S(2)}) copy-start(f32[2,320]{1,0:T(2,128)} %param.24) | copy-start | bytes 7684
  54.3 4.0 %copy-start.17 = (f32[2,320]{1,0:T(2,128)S(1)}, f32[2,320]{1,0:T(2,128)}, u32[]{:S(2)}) copy-start(f32[2,320]{1,0:T(2,128)} %param.23) | copy-start | bytes 7684
  54.3 4.0 %copy-start.21 = (s32[1,2]{1,0:T(1,128)S(1)}, s32[1,2]{1,0:T(1,128)}, u32[]{:S(2)}) copy-start(s32[1,2]{1,0:T(1,128)} %param.18) | copy-start | bytes 28
  54.3 4.3 %copy-start.6 = (bf16[1,2,32,320]{3,2,1,0:T(8,128)(2,1)S(1)}, bf16[1,2,32,320]{3,2,1,0:T(8,128)(2,1)}, u32[]{:S(2)}) copy-start(bf16[1,2,32,320]{3,2,1,0:T(8,128)(2,1)} %param.17) | copy-start | bytes 122884
  54.3 4.3 %copy-start.11 = (bf16[1,2,32,320]{3,2,1,0:T(8,128)(2,1)S(1)}, bf16[1,2,32,320]{3,2,1,0:T(8,128)(2,1)}, u32[]{:S(2)}) copy-start(bf16[1,2,32,320]{3,2,1,0:T(8,128)(2,1)} %param.16) | copy-start | bytes 122884
  59.6 8.3 %copy-start.14 = (f32[64]{0:T(128)}, f32[64]{0:T(128)S(1)}, u32[]{:S(2)}) copy-start(f32[64]{0:T(128)S(1)} %broadcast_multiply_fusion.5) | copy-start | bytes 772
  59.8 2.4 %copy-start.18 = (f32[64]{0:T(128)}, f32[64]{0:T(128)S(1)}, u32[]{:S(2)}) copy-start(f32[64]{0:T(128)S(1)} %add_rsqrt_fusion.1) | copy-start | bytes 772
  104.3 2.9 %copy-start.10 = (bf16[2,3,320,16]{2,3,1,0:T(8,128)(2,1)S(1)}, bf16[2,3,320,16]{2,3,1,0:T(8,128)(2,1)}, u32[]{:S(2)}) copy-start(bf16[2,3,320,16]{2,3,1,0:T(8,128)(2,1)} %param.25) | copy-start | bytes 184324
  104.3 3.1 %copy-start.5 = (f32[1,2,32,320]{3,2,1,0:T(8,128)S(1)}, f32[1,2,32,320]{3,2,1,0:T(8,128)}, u32[]{:S(2)}) copy-start(f32[1,2,32,320]{3,2,1,0:T(8,128)} %get-tuple-element.14) | copy-start | bytes 245764
  104.3 3.9 %copy-start.1 = (bf16[2,320,2560]{1,2,0:T(8,128)(2,1)S(1)}, bf16[2,320,2560]{1,2,0:T(8,128)(2,1)}, u32[]{:S(2)}) copy-start(bf16[2,320,2560]{1,2,0:T(8,128)(2,1)} %all-gather.3.cloned.1.call-done) | copy-start | bytes 9830404
  106.8 1.3 copy-start.13
  107.9 1.4 copy-start.2
  108.2 1.5 copy-start.7
  110.9 0.9 copy-start.9
  110.9 1.6 copy-start.8
  111.3 2.0 %copy-start.22 = (bf16[2,2560,16]{1,2,0:T(8,128)(2,1)S(1)}, bf16[2,2560,16]{1,2,0:T(8,128)(2,1)}, u32[]{:S(2)}) copy-start(bf16[2,2560,16]{1,2,0:T(8,128)(2,1)} %param.28) | copy-start | bytes 491524
  111.5 2.2 %copy-start.15 = (f32[64]{0:T(128)S(1)}, f32[64]{0:T(128)}, u32[]{:S(2)}) copy-start(f32[64]{0:T(128)} %copy-done.14) | copy-start | bytes 772
  111.5 2.2 %copy-start.19 = (f32[64]{0:T(128)S(1)}, f32[64]{0:T(128)}, u32[]{:S(2)}) copy-start(f32[64]{0:T(128)} %copy-done.18) | copy-start | bytes 772
  113.7 46.3 %copy-start.3 = (bf16[256,2048]{1,0:T(8,128)(2,1)S(1)}, bf16[256,2048]{1,0:T(8,128)(2,1)}, u32[]{:S(2)}) copy-start(bf16[256,2048]{1,0:T(8,128)(2,1)} %param.30) | copy-start | bytes 3145732
  113.7 46.3 %copy-start.20 = (f32[256]{0:T(256)S(1)}, f32[256]{0:T(256)}, u32[]{:S(2)}) copy-start(f32[256]{0:T(256)} %param.31) | copy-start | bytes 3076
  (1 other events, 0.6 us)
Sparse Core Ops, SparseCore 0:
  9.5 43.8 all-gather.4
  55.7 48.5 all-gather.2
where the time goes:
time: 168 us
  blocking collectives  87.6 us (52%)
  waiting for transfers between devices  37.9 us (23%)
  between operations  13.9 us (8%)
  matrix products  13.5 us (8%)
  local copies, waits for them, and re-layouts  13 us (8%)
  other arithmetic  1.84 us (1%)
    all_gather x1, waiting for transfers between devices, on_device(): lax.all_gather(weight_ffin, 'corpus', axis=2, tiled=True)  36.5 us
    psum x1, blocking collectives, on_device(): totals = lax.psum(partial_grads, 'corpus')  32.2 us
    all_gather x1, blocking collectives, on_device(): lax.all_gather(weight_in, 'corpus', axis=2, tiled=True)  25 us
    all_gather x1, blocking collectives, on_device(): lax.all_gather(weight_out, 'corpus', axis=2, tiled=True)  19.7 us
    slice x3, local copies, waits for them, and re-layouts, fetch_forward(): return tuple((member[block] for member in gathered))  7.04 us
    all_to_all x1, blocking collectives, on_device(): lax.all_to_all(totals, 'query', split_axis=1, concat_axis=0, tiled=True)  6.35 us
    unnamed x57, local copies, waits for them, and re-layouts  4.61 us
    all_gather x1, blocking collectives, on_device(): preconditioned = lax.all_gather(owned, 'query', axis=1, tiled=True)  4.33 us
  transfers between devices with their start and end apart: 2, of which 1 were waited for; matrix products, arithmetic and copies ran while one was open for 9% of the time, Pallas kernels for 0%

commit v1 on v0

--- a/solution.py
+++ b/solution.py
@@ -182,7 +182,7 @@
                 records[index][0], records[index][1], pairs[index][0], pairs[index][1], samples
             )
     partial_grads = jnp.stack(layers, axis=1)
-    totals = lax.psum(partial_grads, "corpus")
+    totals = jnp.sum(lax.all_gather(partial_grads, "corpus"), axis=0)
     routed = lax.all_to_all(totals, "query", split_axis=1, concat_axis=0, tiled=True)
     owned = jnp.einsum("qlk,lkj->qlj", routed, precond, precision=lax.Precision.HIGHEST).astype(
         jnp.bfloat16

time: 168 us -> 156 us (0.929)
  blocking collectives: 87.6 us -> 75.2 us
    psum x1 -> x0, blocking collectives: 32.2 us -> none  [on_device(): totals = lax.psum(partial_grads, 'corpus')]
    all_gather x0 -> x1, blocking collectives: none -> 19.8 us  [on_device(): totals = jnp.sum(lax.all_gather(partial_grads, 'corpus'), axis=0)]
    unnamed x57 -> x50, local copies, waits for them, and re-layouts: 4.61 us -> 3.95 us
where the time goes in v1:
time: 156 us; the launch traced here: 155 us
  blocking collectives  75.2 us (48%)
  waiting for transfers between devices  38.5 us (25%)
  between operations  13.9 us (9%)
  matrix products  13.5 us (9%)
  local copies, waits for them, and re-layouts  12.4 us (8%)
  other arithmetic  1.85 us (1%)
    all_gather x1, waiting for transfers between devices, on_device(): lax.all_gather(weight_ffin, 'corpus', axis=2, tiled=True)  37.1 us
    all_gather x1, blocking collectives, on_device(): lax.all_gather(weight_in, 'corpus', axis=2, tiled=True)  25 us
    all_gather x1, blocking collectives, on_device(): totals = jnp.sum(lax.all_gather(partial_grads, 'corpus'), axis=0)  19.8 us
    all_gather x1, blocking collectives, on_device(): lax.all_gather(weight_out, 'corpus', axis=2, tiled=True)  19.7 us
    slice x3, local copies, waits for them, and re-layouts, fetch_forward(): return tuple((member[block] for member in gathered))  7.04 us
    all_to_all x1, blocking collectives, on_device(): lax.all_to_all(totals, 'query', split_axis=1, concat_axis=0, tiled=True)  6.35 us
    all_gather x1, blocking collectives, on_device(): preconditioned = lax.all_gather(owned, 'query', axis=1, tiled=True)  4.33 us
    unnamed x50, local copies, waits for them, and re-layouts  3.95 us
  transfers between devices with their start and end apart: 2, of which 1 were waited for; matrix products, arithmetic and copies ran while one was open for 9% of the time, Pallas kernels for 0%

profile of v1, /device:TPU:0, one launch (start us, length us, event | category | flops | bytes accessed | tf_op | source)
XLA Modules:
  0.0 155.3 jit_solution(9686426144238560264)
XLA Ops:
  6.5 0.7 all-gather.6.cloned.1.call-update
  7.3 0.7 all-gather.4.cloned.1.call-update
  8.0 25.0 %all_gather.21 = bf16[2,320,320]{1,0,2:T(2,128)(2,1)S(1)} all-gather(bf16[2,320,20]{1,0,2:T(2,128)(2,1)} %param.19), channel_id=1, replica_groups=mesh['query'=2,'corpus'=16] {'corpus'}, dimensions={2}, use_global_device_ids=true | all-gather | bytes 435200 | tf_op jit(solution)/shard_map/all_gather | solution.py:155
  33.0 0.7 fusion.105
  33.7 0.9 copy.36
  34.6 19.7 %all_gather.24 = bf16[2,320,320]{1,0,2:T(2,128)(2,1)S(1)} all-gather(bf16[2,320,20]{1,0,2:T(2,128)(2,1)S(1)} %copy-done.12), channel_id=1, replica_groups=mesh['query'=2,'corpus'=16] {'corpus'}, dimensions={2}, use_global_device_ids=true | all-gather | bytes 435200 | tf_op jit(solution)/shard_map/all_gather | solution.py:158
  54.3 0.7 fusion.104
  55.0 0.9 copy.38
  55.9 0.9 copy.39
  56.8 0.9 copy.41
  57.7 0.6 slice_reduce_fusion
  58.6 0.7 fusion.102
  59.8 0.8 fusion.79
  60.7 0.9 fusion.76
  61.6 5.7 %fusion.103 = (bf16[1,1280,320]{1,0,2:T(2,128)(2,1)}, bf16[1,1280,320]{1,0,2:T(2,128)(2,1)S(1)}) fusion(bf16[2,1280,320]{1,0,2:T(2,128)(2,1)} %all-gather.6.cloned.1.call-done), kind=kLoop, calls=%fused_computation.153 | loop fusion | bytes 3276800 | tf_op jit(solution)/shard_map/slice | solution.py:162
  67.3 37.1 %all-gather.4.cloned.1.call-done = bf16[2,320,2560]{1,2,0:T(8,128)(2,1)} async-done(((bf16[2,320,160]{1,2,0:T(8,128)(2,1)}), bf16[2,320,2560]{1,2,0:T(8,128)(2,1)}) %all-gather.4.cloned.1.call-update) | async-done | bytes 3276816 | tf_op jit(solution)/shard_map/all_gather | solution.py:156
  104.3 2.5 %fusion.1 = f32[64,2560]{1,0:T(8,128)S(1)} fusion(bf16[64,320]{1,0:T(8,128)(2,1)} %copy-done.4, bf16[2,320,2560]{1,2,0:T(8,128)(2,1)} %all-gather.4.cloned.1.call-done), kind=kOutput, calls=%fused_computation.3 | convolution fusion | flops 104857600 | bytes 2670592 | tf_op jit(solution)/shard_map/dot_general | solution.py:42
  108.2 0.7 fusion.3
  113.7 0.5 fusion.100
  116.3 19.8 %all-gather = f32[16,8,256]{2,1,0:T(8,128)S(1)} all-gather(f32[1,8,256]{2,1,0:T(8,128)S(1)} %stack.3), channel_id=2, replica_groups=mesh['query'=2,'corpus'=16] {'corpus'}, dimensions={0}, use_global_device_ids=true | all-gather | bytes 139264 | tf_op jit(solution)/shard_map/all_gather | solution.py:185
  136.2 6.4 %all_to_all.12 = f32[1,8,256]{2,0,1:T(1,128)S(1)} all-to-all(f32[1,8,256]{2,0,1:T(1,128)S(1)} %reduce_sum.102), channel_id=1, replica_groups=mesh['query'=2,'corpus'=16] {'query'}, dimensions={1} | all-to-all | bytes 16384 | tf_op jit(solution)/shard_map/all_to_all | solution.py:186
  142.6 0.6 fusion.11
  143.2 4.3 %all_gather.27 = bf16[2,8,256]{2,0,1:T(2,128)(2,1)S(1)} all-gather(bf16[2,4,256]{2,0,1:T(2,128)(2,1)S(1)} %fusion.11), channel_id=1, replica_groups=mesh['query'=2,'corpus'=16] {'query'}, dimensions={1}, use_global_device_ids=true | all-gather | bytes 12288 | tf_op jit(solution)/shard_map/all_gather | solution.py:190
  147.5 1.0 convolution_multiply_fusion
  (114 shorter events, 8.9 us)
Async XLA Ops:
  6.5 136.0 %copy-start = (f32[4,256,256]{2,1,0:T(8,128)S(1)}, f32[4,256,256]{2,1,0:T(8,128)}, u32[]{:S(2)}) copy-start(f32[4,256,256]{2,1,0:T(8,128)} %param.29) | copy-start | bytes 3145732
  6.5 28.1 %copy-start.12 = (bf16[2,320,20]{1,0,2:T(2,128)(2,1)S(1)}, bf16[2,320,20]{1,0,2:T(2,128)(2,1)}, u32[]{:S(2)}) copy-start(bf16[2,320,20]{1,0,2:T(2,128)(2,1)} %param.22) | copy-start | bytes 76804
  6.5 55.0 %all-gather.6.cloned.1.call-start = ((), (), s32[]{:S(2)}) async-start(), calls=%async_computation.2 | async-start | bytes 1740800 | tf_op jit(solution)/shard_map/all_gather | solution.py:157
  7.3 97.1 %all-gather.4.cloned.1.call-start = ((), (), s32[]{:S(2)}) async-start(), calls=%async_computation.1 | async-start | bytes 4177920 | tf_op jit(solution)/shard_map/all_gather | solution.py:156
  54.3 3.4 %copy-start.16 = (f32[2,320]{1,0:T(2,128)S(1)}, f32[2,320]{1,0:T(2,128)}, u32[]{:S(2)}) copy-start(f32[2,320]{1,0:T(2,128)} %param.24) | copy-start | bytes 7684
  54.3 4.0 %copy-start.17 = (f32[2,320]{1,0:T(2,128)S(1)}, f32[2,320]{1,0:T(2,128)}, u32[]{:S(2)}) copy-start(f32[2,320]{1,0:T(2,128)} %param.23) | copy-start | bytes 7684
  54.3 4.0 %copy-start.21 = (s32[1,2]{1,0:T(1,128)S(1)}, s32[1,2]{1,0:T(1,128)}, u32[]{:S(2)}) copy-start(s32[1,2]{1,0:T(1,128)} %param.18) | copy-start | bytes 28
  54.3 4.3 %copy-start.6 = (bf16[1,2,32,320]{3,2,1,0:T(8,128)(2,1)S(1)}, bf16[1,2,32,320]{3,2,1,0:T(8,128)(2,1)}, u32[]{:S(2)}) copy-start(bf16[1,2,32,320]{3,2,1,0:T(8,128)(2,1)} %param.17) | copy-start | bytes 122884
  54.3 4.3 %copy-start.11 = (bf16[1,2,32,320]{3,2,1,0:T(8,128)(2,1)S(1)}, bf16[1,2,32,320]{3,2,1,0:T(8,128)(2,1)}, u32[]{:S(2)}) copy-start(bf16[1,2,32,320]{3,2,1,0:T(8,128)(2,1)} %param.16) | copy-start | bytes 122884
  59.6 1.0 copy-start.14
  59.8 7.5 %copy-start.18 = (f32[64]{0:T(128)}, f32[64]{0:T(128)S(1)}, u32[]{:S(2)}) copy-start(f32[64]{0:T(128)S(1)} %add_rsqrt_fusion.1) | copy-start | bytes 772
  104.3 2.9 %copy-start.10 = (bf16[2,3,320,16]{2,3,1,0:T(8,128)(2,1)S(1)}, bf16[2,3,320,16]{2,3,1,0:T(8,128)(2,1)}, u32[]{:S(2)}) copy-start(bf16[2,3,320,16]{2,3,1,0:T(8,128)(2,1)} %param.25) | copy-start | bytes 184324
  104.3 3.1 %copy-start.5 = (f32[1,2,32,320]{3,2,1,0:T(8,128)S(1)}, f32[1,2,32,320]{3,2,1,0:T(8,128)}, u32[]{:S(2)}) copy-start(f32[1,2,32,320]{3,2,1,0:T(8,128)} %get-tuple-element.14) | copy-start | bytes 245764
  104.3 3.9 %copy-start.1 = (bf16[2,320,2560]{1,2,0:T(8,128)(2,1)S(1)}, bf16[2,320,2560]{1,2,0:T(8,128)(2,1)}, u32[]{:S(2)}) copy-start(bf16[2,320,2560]{1,2,0:T(8,128)(2,1)} %all-gather.4.cloned.1.call-done) | copy-start | bytes 9830404
  106.8 1.3 copy-start.13
  107.9 1.4 copy-start.2
  108.2 1.5 copy-start.7
  110.9 0.9 copy-start.9
  110.9 1.6 %copy-start.8 = (bf16[2,1280,16]{1,2,0:T(8,128)(2,1)S(1)}, bf16[2,1280,16]{1,2,0:T(8,128)(2,1)}, u32[]{:S(2)}) copy-start(bf16[2,1280,16]{1,2,0:T(8,128)(2,1)} %param.26) | copy-start | bytes 245764
  111.3 2.0 %copy-start.22 = (bf16[2,2560,16]{1,2,0:T(8,128)(2,1)S(1)}, bf16[2,2560,16]{1,2,0:T(8,128)(2,1)}, u32[]{:S(2)}) copy-start(bf16[2,2560,16]{1,2,0:T(8,128)(2,1)} %param.28) | copy-start | bytes 491524
  111.5 2.2 %copy-start.15 = (f32[64]{0:T(128)S(1)}, f32[64]{0:T(128)}, u32[]{:S(2)}) copy-start(f32[64]{0:T(128)} %copy-done.14) | copy-start | bytes 772
  111.5 2.2 %copy-start.19 = (f32[64]{0:T(128)S(1)}, f32[64]{0:T(128)}, u32[]{:S(2)}) copy-start(f32[64]{0:T(128)} %copy-done.18) | copy-start | bytes 772
  113.7 33.8 %copy-start.3 = (bf16[256,2048]{1,0:T(8,128)(2,1)S(1)}, bf16[256,2048]{1,0:T(8,128)(2,1)}, u32[]{:S(2)}) copy-start(bf16[256,2048]{1,0:T(8,128)(2,1)} %param.30) | copy-start | bytes 3145732
  113.7 33.8 %copy-start.20 = (f32[256]{0:T(256)S(1)}, f32[256]{0:T(256)}, u32[]{:S(2)}) copy-start(f32[256]{0:T(256)} %param.31) | copy-start | bytes 3076
  (1 other events, 0.9 us)
Sparse Core Ops, SparseCore 0:
  9.5 43.8 all-gather.5
  55.7 48.5 all-gather.3
